TPU v7x, 256 devices: a whole 4x4x8 slice. The times are simulated.
256 devices in a mesh: rows: 64 (over x, z_hi, y), rep: 4 (over z_lo, core).
Axes of the slice: x: 4, y: 4, z: 8 (z_hi: 4, z_lo: 2; z = z_hi * 2 + z_lo), core: 2. Of those that a mesh axis runs over, the one named last changes fastest.
Arguments:
- features: float32 [32768, 256], P(('rows', 'rep')), may hold values from -6 to 6
- weight: float32 [256, 256], replicated, may hold values from -0.375 to 0.375
- cotangent: float32 [32768, 256], P(('rows', 'rep')), may hold values from -6 to 6
- tiles: float32 [64, 4, 64, 2, 128, 128], P('rows', 'rep'), may hold values from -0.046875 to 0.046875
- tile_count: int32 [64, 4, 64], P('rows', 'rep'), may hold values from 0 to 2, as said below
- tile_block: int32 [64, 4, 64, 2], P('rows', 'rep'), may hold values from 0 to 3, as said below
Outputs:
- hidden: float32 [32768, 256], P(('rows', 'rep'))
- grad_weight: float32 [256, 256], replicated
- grad_features: float32 [32768, 256], P(('rows', 'rep'))
Inputs may be any that keep to these rules, and one draw needn't show every extreme that they name: `tile_count`: at the section equal to the row group, every column block holds 2 live tiles. `tile_block`: the blocks named by one section's slots are distinct; slots at or beyond the section's count are ignored.
All inputs are finite; a program needn't handle non-finite values.
Results may differ from a plain program's by a relative error of at most 0.0001.
Values sent between devices are 32-bit elements; how exact they have to be, the bound alone decides.
No kernel may reach another device: no remote copies, remote signals or barrier semaphores. Data moves between devices by JAX's collectives and lax.ppermute only.
A program may use at most 128 MiB of HBM per device.

v0:
```python
import math

import jax
import jax.numpy as jnp
from jax import lax
from jax.sharding import PartitionSpec as P


def silu_slope(pre):
    sig = jax.nn.sigmoid(pre)
    return sig * (1.0 + pre * (1.0 - sig))


def body(features, weight, cotangent, tiles, tile_count, tile_block):
    highest = lax.Precision.HIGHEST
    tile_set = tiles[0, 0]
    counts = tile_count[0, 0]
    block_ids = tile_block[0, 0]
    sections = tile_set.shape[0]
    slots = tile_set.shape[1]
    blk = tile_set.shape[2]
    width = features.shape[1]
    groups = lax.axis_size("rep")
    select = (
        (block_ids[..., None] == jnp.arange(groups, dtype=jnp.int32))
        & (jnp.arange(slots, dtype=jnp.int32)[:, None] < counts[:, None, None])
    ).astype(jnp.float32)
    gathered = lax.all_gather(features, "rows", axis=0, tiled=True).reshape(sections, blk, width)
    prods = jnp.einsum("stab,sbf->staf", tile_set, gathered, precision=highest)
    total = jnp.einsum("stk,staf->kaf", select, prods, precision=highest)
    aggregated = lax.psum_scatter(
        total.reshape(groups * blk, width), "rep", scatter_dimension=0, tiled=True
    )
    pre = jnp.dot(aggregated, weight, precision=highest)
    hidden = jax.nn.silu(pre)
    delta = cotangent * silu_slope(pre)
    weight_term = jnp.dot(aggregated.T, delta, precision=highest)
    node_total = blk * lax.axis_size("rows") * groups
    grad_weight = lax.psum(weight_term, ("rows", "rep")) / math.sqrt(node_total)
    back = jnp.dot(delta, weight.T, precision=highest)
    group_back = lax.all_gather(back, "rep", axis=0, tiled=True).reshape(groups, blk, width)
    count = sections * blk
    picked = jnp.einsum("stk,kaf->staf", select, group_back, precision=highest)
    result = jnp.einsum("stab,staf->sbf", tile_set, picked, precision=highest)
    all_terms = result.reshape(count, width)
    grad_features = lax.psum_scatter(all_terms, "rows", scatter_dimension=0, tiled=True)
    return (hidden, grad_weight, grad_features)


def solution(mesh):
    in_specs = (
        P(("rows", "rep"), None),
        P(),
        P(("rows", "rep"), None),
        P("rows", "rep", None, None, None, None),
        P("rows", "rep", None),
        P("rows", "rep", None, None),
    )
    out_specs = (P(("rows", "rep"), None), P(), P(("rows", "rep"), None))
    return jax.shard_map(body, mesh=mesh, in_specs=in_specs, out_specs=out_specs, check_vma=False)
```

profile of v0, /device:TPU:64, one launch (start us, length us, event | category | flops | bytes accessed | tf_op | source)
XLA Modules:
  0.0 852.2 jit_solution(4370416424128967290)
XLA Ops:
  7.2 0.0 copy-start
  7.2 0.0 all-gather.2.cloned.1.call-start
  7.2 0.7 all-gather.2.cloned.1.call-update
  7.9 0.0 reduce-scatter.3.cloned.1.call-start
  8.0 0.7 iota_compare_fusion.1
  8.6 119.7 %all-gather.2.cloned.1.call-done = f32[8192,256]{1,0:T(8,128)} async-done(((f32[128,256]{1,0:T(8,128)}), f32[8192,256]{1,0:T(8,128)}) %all-gather.2.cloned.1.call-update) | async-done | bytes 8388624 | tf_op jit(solution)/shard_map/all_gather | solution.py:28
  128.3 0.0 copy-start.1
  128.3 23.4 %fusion.5 = f32[64,2,128,256]{3,2,1,0:T(8,128)} fusion(f32[64,128,256,1]{2,1,3,0:T(8,128)} %bitcast.38, f32[1,1,64,2,128,128]{5,4,3,2,1,0:T(8,128)} %param.9), kind=kOutput, calls=%fused_computation.5 | convolution fusion | flops 6442450944 | bytes 33554432 | tf_op jit(solution)/shard_map/stab,sbf->staf/dot_general | solution.py:29
  151.7 0.0 copy-done.1
  151.7 0.0 copy-start.2
  151.7 20.2 %fusion.7 = f32[4,128,256]{2,0,1:T(4,128)S(1)} fusion(f32[64,2,128,256]{3,2,1,0:T(8,128)} %fusion.5, s32[64,2]{0,1:T(2,128)S(1)} %bitcast.41, pred[64,2]{0,1:T(4,128)(4,1)S(1)} %iota_compare_fusion.1), kind=kOutput, calls=%fused_computation.7 | convolution fusion | flops 201327616 | bytes 17302144 | tf_op jit(solution)/shard_map/stk,staf->kaf/dot_general | solution.py:30
  171.9 0.9 copy.10
  172.8 0.0 reduce-scatter.3.cloned.1.call-update
  172.8 0.0 all-reduce.2.cloned.1.call-start
  172.9 19.2 %reduce-scatter.3.cloned.1.call-done = f32[128,256]{1,0:T(8,128)} async-done(((f32[512,256]{1,0:T(8,128)}), f32[128,256]{1,0:T(8,128)}) %reduce-scatter.3.cloned.1.call-update) | async-done | bytes 131088 | tf_op jit(solution)/shard_map/reduce_scatter | solution.py:31
  192.1 0.0 copy-done
  192.1 1.9 fusion.12
  194.0 0.0 copy-done.2
  194.0 0.4 fusion.22
  194.4 2.0 fusion.23
  196.4 0.0 all-reduce.2.cloned.1.call-update
  196.4 0.0 reduce-scatter.5.cloned.1.call-start
  196.5 7.3 all_gather.7
  203.8 9.6 %fusion.10 = f32[64,2,128,256]{3,0,2,1:T(8,128)} fusion(f32[4,128,256,1]{2,1,0,3:T(8,128)S(1)} %bitcast.39, s32[64,2]{0,1:T(2,128)S(1)} %bitcast.42, pred[64,2]{0,1:T(4,128)(4,1)S(1)} %iota_compare_fusion.1), kind=kOutput, calls=%fused_computation.8 | convolution fusion | flops 201327616 | bytes 17302144 | tf_op jit(solution)/shard_map/stk,kaf->staf/dot_general | solution.py:43
  213.4 32.2 %fusion = f32[64,256,128,1]{1,2,3,0:T(8,128)} fusion(f32[64,2,128,256]{3,0,2,1:T(8,128)} %fusion.10, f32[1,1,64,2,128,128]{5,4,3,2,1,0:T(8,128)} %param.9), kind=kOutput, calls=%fused_computation | convolution fusion | flops 6442450944 | bytes 33554432 | tf_op jit(solution)/shard_map/stab,staf->sbf/dot_general | solution.py:44
  245.6 0.0 reduce-scatter.5.cloned.1.call-update
  245.7 200.6 %all-reduce.2.cloned.1.call-done = f32[256,256]{1,0:T(8,128)} async-done(((f32[256,256]{1,0:T(8,128)}), f32[256,256]{1,0:T(8,128)}) %all-reduce.2.cloned.1.call-update) | async-done | bytes 262160 | tf_op jit(solution)/shard_map/psum | solution.py:39
  446.3 1.7 broadcast_multiply_fusion
  447.9 397.7 %reduce-scatter.5.cloned.1.call-done = f32[128,256]{1,0:T(8,128)} async-done(((f32[8192,256]{1,0:T(8,128)}), f32[128,256]{1,0:T(8,128)}) %reduce-scatter.5.cloned.1.call-update) | async-done | bytes 131088 | tf_op jit(solution)/shard_map/reduce_scatter | solution.py:46
Async XLA Ops:
  7.2 184.9 %copy-start = (f32[256,256]{1,0:T(8,128)S(1)}, f32[256,256]{1,0:T(8,128)}, u32[]{:S(2)}) copy-start(f32[256,256]{1,0:T(8,128)} %param.7) | copy-start | bytes 786436
  7.2 121.1 %all-gather.2.cloned.1.call-start = ((), (), s32[]{:S(2)}) async-start(), calls=%async_computation.2 | async-start | bytes 8519680 | tf_op jit(solution)/shard_map/all_gather | solution.py:28
  7.9 184.2 %reduce-scatter.3.cloned.1.call-start = ((), (), s32[]{:S(2)}) async-start(), calls=%async_computation.3 | async-start | bytes 655360 | tf_op jit(solution)/shard_map/reduce_scatter | solution.py:31
  128.3 23.4 %copy-start.1 = (s32[1,1,64,2]{2,3,1,0:T(2,128)S(1)}, s32[1,1,64,2]{2,3,1,0:T(2,128)}, u32[]{:S(2)}) copy-start(s32[1,1,64,2]{2,3,1,0:T(2,128)} %param.11) | copy-start | bytes 1540
  151.7 42.3 %copy-start.2 = (f32[128,256]{1,0:T(8,128)S(1)}, f32[128,256]{1,0:T(8,128)}, u32[]{:S(2)}) copy-start(f32[128,256]{1,0:T(8,128)} %param.8) | copy-start | bytes 393220
  172.8 273.4 %all-reduce.2.cloned.1.call-start = ((), (), s32[]{:S(2)}) async-start(), calls=%async_computation.4 | async-start | bytes 524288 | tf_op jit(solution)/shard_map/psum | solution.py:39
  196.4 649.2 %reduce-scatter.5.cloned.1.call-start = ((), (), s32[]{:S(2)}) async-start(), calls=%async_computation.5 | async-start | bytes 8519680 | tf_op jit(solution)/shard_map/reduce_scatter | solution.py:46
Sparse Core Ops, SparseCore 0:
  11.3 116.9 all-gather.1
  173.0 19.0 reduce-scatter.2
  198.1 248.0 all-reduce.1
  449.2 396.3 reduce-scatter.4
where the time goes:
time: 864 us; the launch traced here: 852 us
  waiting for transfers between devices  738 us (85%)
  matrix products  89.7 us (10%)
  between operations  13.8 us (2%)
    reduce_scatter x1, waiting for transfers between devices, body(): lax.psum_scatter(all_terms, 'rows', scatter_dimension=0, tiled=True)  398 us
    psum x1, waiting for transfers between devices, body(): grad_weight = lax.psum(weight_term, ('rows', 'rep')) / math.sqrt(node_total)  201 us
    all_gather x1, waiting for transfers between devices, body(): lax.all_gather(features, 'rows', axis=0, tiled=True)  120 us
    dot_general x1, matrix products, body(): result = jnp.einsum('stab,staf->sbf', tile_set, picked, precision=highest)  32.2 us
    dot_general x1, matrix products, body(): prods = jnp.einsum('stab,sbf->staf', tile_set, gathered, precision=highest)  23.4 us
    dot_general x1, matrix products, body(): total = jnp.einsum('stk,staf->kaf', select, prods, precision=highest)  20.2 us
    reduce_scatter x1, waiting for transfers between devices, body(): lax.psum_scatter(total.reshape(groups * blk, width), 'rep', scatter_dimen...  19.2 us
  transfers between devices with their start and end apart: 4, of which 4 were waited for; matrix products, arithmetic and copies ran while one was open for 5% of the time, Pallas kernels for 0%

commit v1 on v0

v1 whole, which is shorter than its diff:
```python
import functools
import math

import jax
import jax.numpy as jnp
from jax import lax
from jax.experimental import pallas as pl
from jax.experimental.pallas import tpu as pltpu
from jax.sharding import PartitionSpec as P

SIDE = 4
F32 = jnp.float32
BF16 = jnp.bfloat16


def row_index(x, z, y):
    return (x * SIDE + z) * SIDE + y


def toward(axis, step):
    pairs = []
    for x in range(SIDE):
        for z in range(SIDE):
            for y in range(SIDE):
                at = [x, z, y]
                at["xzy".index(axis)] = (at["xzy".index(axis)] + step) % SIDE
                pairs.append((row_index(x, z, y), row_index(*at)))
    return pairs


def send(value, axis, step):
    return lax.ppermute(value, "rows", toward(axis, step))


def swap(value, bit):
    return lax.ppermute(value, "rep", [(r, r ^ bit) for r in range(4)])


def split(value):
    high = value.astype(BF16)
    return high, (value - high.astype(F32)).astype(BF16)


def mm(left, right):
    return jnp.dot(left, right, preferred_element_type=F32)


def panel_kernel(at_ref, count_ref, block_ref, tiles_ref, high_ref, low_ref):
    x = lax.rem(at_ref[0] + pl.program_id(0), SIDE)
    z = lax.rem(at_ref[1] + pl.program_id(1), SIDE)
    for dy in range(SIDE):
        y = lax.rem(at_ref[2] + dy, SIDE)
        section = row_index(x, z, y)
        count = count_ref[section]
        first, second = block_ref[2 * section], block_ref[2 * section + 1]
        for k in range(4):
            w0 = jnp.where((first == k) & (count > 0), 1.0, 0.0).astype(F32)
            w1 = jnp.where((second == k) & (count > 1), 1.0, 0.0).astype(F32)
            high, low = split(tiles_ref[0, 0, y, 0] * w0 + tiles_ref[0, 0, y, 1] * w1)
            high_ref[0, dy, 0, pl.ds(k * 128, 128), :] = high
            low_ref[0, dy, 0, pl.ds(k * 128, 128), :] = low


def make_panel(at, counts, blocks, tiles):
    shape = jax.ShapeDtypeStruct((SIDE, SIDE, SIDE, 512, 128), BF16)
    out_spec = pl.BlockSpec((1, SIDE, 1, 512, 128), lambda i, j, at, c, b: (i, 0, j, 0, 0))
    return pl.pallas_call(
        panel_kernel,
        grid_spec=pltpu.PrefetchScalarGridSpec(
            num_scalar_prefetch=3,
            grid=(SIDE, SIDE),
            in_specs=[
                pl.BlockSpec(
                    (1, 1, SIDE, 2, 128, 128),
                    lambda i, j, at, c, b: (
                        lax.rem(at[0] + i, SIDE),
                        lax.rem(at[1] + j, SIDE),
                        0,
                        0,
                        0,
                        0,
                    ),
                )
            ],
            out_specs=[out_spec, out_spec],
        ),
        out_shape=[shape, shape],
        cost_estimate=pl.CostEstimate(flops=10**8, bytes_accessed=25 * 10**6, transcendentals=0),
        compiler_params=pltpu.CompilerParams(vmem_limit_bytes=32 * 2**20),
        name="panel",
    )(at, counts, blocks, tiles.reshape(SIDE, SIDE, SIDE, 2, 128, 128))


def panel_spec(half, pick):
    def index(i):
        d, o = pick(i)
        return (d, o, 0, 0, 0) if half == 0 else (o, d, 0, 0, 0)

    return pl.BlockSpec((1, 1, SIDE, 512, 128), index)


def wide(ref):
    return jnp.concatenate([ref[0, 0, dz] for dz in range(SIDE)], axis=1)


def forward_kernel(halves, *refs):
    n = len(halves)
    highs, lows, blocks = refs[:n], refs[n : 2 * n], refs[2 * n : 3 * n]
    starts, totals = refs[3 * n : 3 * n + 2], refs[3 * n + 2 :]

    @pl.when(pl.program_id(0) == 0)
    def _():
        for start, total in zip(starts, totals):
            total[...] = start[...]

    for half, high, low, block in zip(halves, highs, lows, blocks):
        g_high, g_low = split(block[0].reshape(SIDE * 128, 128))
        both = mm(wide(high), jnp.concatenate([g_high, g_low], axis=1))
        totals[half][...] += both[:, :128] + (both[:, 128:] + mm(wide(low), g_high))


def forward(panel, totals, steps, jobs):
    whole = pl.BlockSpec((512, 128), lambda i: (0, 0))
    specs = [panel_spec(half, pick) for half, pick, _ in jobs]
    return pl.pallas_call(
        functools.partial(forward_kernel, [half for half, _, _ in jobs]),
        grid=(steps,),
        in_specs=specs
        + specs
        + [pl.BlockSpec((1, SIDE, 128, 128), lambda i: (i, 0, 0, 0)) for _ in jobs]
        + [whole, whole],
        out_specs=[whole, whole],
        out_shape=[jax.ShapeDtypeStruct((512, 128), F32)] * 2,
        cost_estimate=pl.CostEstimate(
            flops=len(jobs) * steps * 4 * 2 * 512 * 512 * 128,
            bytes_accessed=len(jobs) * steps * 13 * 10**5,
            transcendentals=0,
        ),
        compiler_params=pltpu.CompilerParams(vmem_limit_bytes=48 * 2**20),
        name="forward",
    )(*[panel[0]] * len(jobs), *[panel[1]] * len(jobs), *[array for _, _, array in jobs], *totals)


def middle_kernel(own_ref, other_ref, weight_ref, cot_ref, hidden_ref, term_ref, back_ref):
    highest = lax.Precision.HIGHEST
    aggregated = own_ref[...] + other_ref[...]
    weight = weight_ref[...]
    pre = jnp.dot(aggregated, weight, precision=highest, preferred_element_type=F32)
    sig = 1.0 / (1.0 + jnp.exp(-pre))
    hidden_ref[...] = pre * sig
    delta = cot_ref[...] * (sig * (1.0 + pre * (1.0 - sig)))
    back_ref[...] = lax.dot_general(
        weight, delta, (((1,), (1,)), ((), ())), precision=highest, preferred_element_type=F32
    )
    term_ref[...] = jnp.dot(aggregated.T, delta, precision=highest, preferred_element_type=F32)


def middle(own, other, weight, cotangent):
    return pl.pallas_call(
        middle_kernel,
        out_shape=[
            jax.ShapeDtypeStruct((128, 256), F32),
            jax.ShapeDtypeStruct((256, 256), F32),
            jax.ShapeDtypeStruct((256, 128), F32),
        ],
        compiler_params=pltpu.CompilerParams(vmem_limit_bytes=32 * 2**20),
        name="middle",
    )(own, other, weight, cotangent)


def backward_kernel(halves, back_ref, *refs):
    n = len(halves)
    highs, lows, outs = refs[:n], refs[n : 2 * n], refs[2 * n :]
    for half, high, low, out in zip(halves, highs, lows, outs):
        back = jnp.concatenate([back_ref[k, pl.ds(half * 128, 128), :] for k in range(4)], axis=1)
        b_high, b_low = split(back)
        both = mm(jnp.concatenate([b_high, b_low], axis=0), wide(high))
        result = both[:128] + (both[128:] + mm(b_high, wide(low)))
        for dz in range(SIDE):
            out[0, dz] = result[:, dz * 128 : (dz + 1) * 128]


def backward(panel, back, steps, jobs):
    specs = [panel_spec(half, pick) for half, pick in jobs]
    return pl.pallas_call(
        functools.partial(backward_kernel, [half for half, _ in jobs]),
        grid=(steps,),
        in_specs=[pl.BlockSpec((4, 256, 128), lambda i: (0, 0, 0))] + specs + specs,
        out_specs=[pl.BlockSpec((1, SIDE, 128, 128), lambda i: (i, 0, 0, 0)) for _ in jobs],
        out_shape=[jax.ShapeDtypeStruct((steps, SIDE, 128, 128), F32) for _ in jobs],
        cost_estimate=pl.CostEstimate(
            flops=len(jobs) * steps * 4 * 2 * 512 * 512 * 128,
            bytes_accessed=len(jobs) * steps * 13 * 10**5,
            transcendentals=0,
        ),
        compiler_params=pltpu.CompilerParams(vmem_limit_bytes=48 * 2**20),
        name="backward",
    )(back, *[panel[0]] * len(jobs), *[panel[1]] * len(jobs))


BIG = ("x", "y")
MID = ("y", "x")


def gather_forward(features, panel):
    two = jnp.stack([features[:, :128], features[:, 128:]])
    by_z = [two] + [send(two, "z", -d) for d in (1, 2, 3)]
    totals = [jnp.zeros((512, 128), F32)] * 2
    near = []
    for half in range(2):
        mine = jnp.stack([block[half] for block in by_z])
        near.append(jnp.stack([mine] + [send(mine, MID[half], -d) for d in (1, 2, 3)]))
    first = [(send(near[h], BIG[h], -1), send(near[h], BIG[h], 1)) for h in range(2)]
    second = [
        (send(first[h][0][:2], BIG[h], -1), send(first[h][1][2:], BIG[h], 1)) for h in range(2)
    ]
    totals = forward(panel, totals, 4, [(h, lambda i: (0, i), near[h]) for h in range(2)])
    totals = forward(
        panel,
        totals,
        4,
        [(h, lambda i, d=d: (d, i), first[h][j]) for h in range(2) for j, d in enumerate((1, 3))],
    )
    return forward(
        panel,
        totals,
        2,
        [(h, lambda i, j=j: (2, 2 * j + i), second[h][j]) for h in range(2) for j in range(2)],
    )


def scatter_backward(back, panel):
    early = backward(
        panel,
        back,
        4,
        [
            (h, pick)
            for h in range(2)
            for pick in (
                lambda i: (1 + i // 2, (i + 2) % 4),
                lambda i: (3 - i // 2, i),
            )
        ],
    )
    late = backward(
        panel,
        back,
        2,
        [
            (h, pick)
            for h in range(2)
            for pick in (
                lambda i: (1, i),
                lambda i: (3, i + 2),
                lambda i: (0, i),
                lambda i: (0, i + 2),
            )
        ],
    )
    by_half = []
    for h in range(2):
        up, down = early[2 * h], early[2 * h + 1]
        late_up, late_down, own_a, own_b = late[4 * h : 4 * h + 4]
        from_below, from_above = send(up, BIG[h], 1), send(down, BIG[h], -1)
        relay_up = send(late_up + from_below[2:], BIG[h], 1)
        relay_down = send(late_down + from_above[2:], BIG[h], -1)
        part_a = own_a + from_above[:2] + relay_up
        part_b = own_b + from_below[:2] + relay_down
        by_half.append(
            part_a[0]
            + send(part_a[1], MID[h], 1)
            + send(part_b[0], MID[h], 2)
            + send(part_b[1], MID[h], 3)
        )
    both = jnp.stack(by_half, axis=1)
    total = both[0] + send(both[1], "z", 1) + send(both[2], "z", 2) + send(both[3], "z", 3)
    return total.reshape(256, 128).T


def pick_two(value, r):
    core, low = r % 2, r // 2
    kept = lax.dynamic_index_in_dim(value, core, 1, keepdims=False)
    given = lax.dynamic_index_in_dim(value, 1 - core, 1, keepdims=False)
    pair = kept + swap(given, 1)
    mine = lax.dynamic_index_in_dim(pair, low, 0, keepdims=False)
    return mine, swap(lax.dynamic_index_in_dim(pair, 1 - low, 0, keepdims=False), 2)


def body(features, weight, cotangent, tiles, tile_count, tile_block):
    g, r = lax.axis_index("rows"), lax.axis_index("rep")
    at = jnp.stack([g // 16, (g // 4) % 4, g % 4]).astype(jnp.int32)
    panel = make_panel(at, tile_count.reshape(-1), tile_block.reshape(-1), tiles[0, 0])
    totals = gather_forward(features, panel)
    partial = jnp.concatenate(totals, axis=1).reshape(2, 2, 128, 256)
    own, other = pick_two(partial, r)
    hidden, term, back = middle(own, other, weight, cotangent)
    back = lax.all_gather(back, "rep", axis=0, tiled=False)
    grad_features = scatter_backward(back, panel)
    mine, theirs = pick_two(term.reshape(2, 2, 64, 256), r)
    piece = mine + theirs
    for axis in "zyx":
        piece = (piece + send(piece, axis, 2)) + (send(piece, axis, 1) + send(piece, axis, 3))
    node_total = 128 * lax.axis_size("rows") * lax.axis_size("rep")
    grad_weight = lax.all_gather(piece, "rep", axis=0, tiled=True) / math.sqrt(node_total)
    return hidden, grad_weight, grad_features


def solution(mesh):
    in_specs = (
        P(("rows", "rep"), None),
        P(),
        P(("rows", "rep"), None),
        P("rows", "rep", None, None, None, None),
        P("rows", "rep", None),
        P("rows", "rep", None, None),
    )
    out_specs = (P(("rows", "rep"), None), P(), P(("rows", "rep"), None))
    return jax.shard_map(body, mesh=mesh, in_specs=in_specs, out_specs=out_specs, check_vma=False)
```

time: 864 us -> 255 us (0.30)
  the two profiles are of different devices: /device:TPU:64 before, /device:TPU:1 now
where the time goes in v1:
time: 255 us; the launch traced here: 250 us
  starting transfers between devices  79.1 us (31%)
  waiting for transfers between devices  77.2 us (30%)
  Pallas kernels  51.6 us (20%)
  blocking collectives  25.4 us (10%)
  local copies, waits for them, and re-layouts  13.3 us (5%)
    ppermute x43, starting transfers between devices, send(): return lax.ppermute(value, 'rows', toward(axis, step))  74.4 us
    ppermute x43, waiting for transfers between devices, send(): return lax.ppermute(value, 'rows', toward(axis, step))  71.3 us
    pallas_call x3, Pallas kernels, forward(): pl.pallas_call(functools.partial(forward_kernel, [half for half, _, _ in...  20.9 us
    all_gather x1, blocking collectives, body(): lax.all_gather(piece, 'rep', axis=0, tiled=True) / math.sqrt(node_total)  18.1 us
    pallas_call x2, Pallas kernels, backward(): pl.pallas_call(functools.partial(backward_kernel, [half for half, _ in jo...  17.7 us
    pallas_call x1, Pallas kernels, make_panel(): pl.pallas_call(panel_kernel, grid_spec=pltpu.PrefetchScalarGridSpec(num_s...  11.9 us
    unnamed x11, local copies, waits for them, and re-layouts  8.03 us
    all_gather x1, blocking collectives, body(): back = lax.all_gather(back, 'rep', axis=0, tiled=False)  7.28 us
  transfers between devices with their start and end apart: 47, of which 19 were waited for; matrix products, arithmetic and copies ran while one was open for 2% of the time, Pallas kernels for 18%

profile of v1, /device:TPU:1, one launch (start us, length us, event | category | flops | bytes accessed | tf_op | source)
XLA Modules:
  0.0 249.8 jit_solution(13698816120162918713)
XLA Ops:
  1.5 3.9 %collective-permute-start.2 = (f32[2,128,128]{2,1,0:T(8,128)S(1)}, f32[2,128,128]{2,1,0:T(8,128)S(1)}, u32[]{:S(2)}, u32[]{:S(2)}) collective-permute-start(f32[2,128,128]{2,1,0:T(8,128)S(1)} %pad_maximum_fusion.6), channel_id=1, source_target_pairs={{0,16},{4,20},{8,24},{12,28},{16,32},{20,36},{24,40},{28,44},{32,4... | collective-permute-start | bytes 393224 | tf_op jit(solution)/shard_map/ppermute | solution.py:32
  5.4 5.1 %collective-permute-start.1 = (f32[2,128,128]{2,1,0:T(8,128)S(1)}, f32[2,128,128]{2,1,0:T(8,128)S(1)}, u32[]{:S(2)}, u32[]{:S(2)}) collective-permute-start(f32[2,128,128]{2,1,0:T(8,128)S(1)} %pad_maximum_fusion.6), channel_id=1, source_target_pairs={{0,32},{4,36},{8,40},{12,44},{16,48},{20,52},{24,56},{28,60},{32,0... | collective-permute-start | bytes 393224 | tf_op jit(solution)/shard_map/ppermute | solution.py:32
  10.5 2.4 collective-permute-start
  12.9 6.2 %collective-permute-done.1 = f32[2,128,128]{2,1,0:T(8,128)S(1)} collective-permute-done((f32[2,128,128]{2,1,0:T(8,128)S(1)}, f32[2,128,128]{2,1,0:T(8,128)S(1)}, u32[]{:S(2)}, u32[]{:S(2)}) %collective-permute-start.1) | collective-permute-done | bytes 131104 | tf_op jit(solution)/shard_map/ppermute | solution.py:32
  19.2 4.3 %collective-permute-done = f32[2,128,128]{2,1,0:T(8,128)S(1)} collective-permute-done((f32[2,128,128]{2,1,0:T(8,128)S(1)}, f32[2,128,128]{2,1,0:T(8,128)S(1)}, u32[]{:S(2)}, u32[]{:S(2)}) %collective-permute-start) | collective-permute-done | bytes 131104 | tf_op jit(solution)/shard_map/ppermute | solution.py:32
  23.5 3.0 %collective-permute-start.4 = (f32[4,128,128]{2,1,0:T(8,128)S(1)}, f32[4,128,128]{2,1,0:T(8,128)S(1)}, u32[]{:S(2)}, u32[]{:S(2)}) collective-permute-start(f32[4,128,128]{2,1,0:T(8,128)S(1)} %get-tuple-element.65), channel_id=1, source_target_pairs={{0,8},{4,12},{8,0},{12,4},{16,24},{20,28},{24,16},{28,20},{32,40},... | collective-permute-start | bytes 786440 | tf_op jit(solution)/shard_map/ppermute | solution.py:32
  28.0 2.8 %collective-permute-start.11 = (f32[4,128,128]{2,1,0:T(8,128)S(1)}, f32[4,128,128]{2,1,0:T(8,128)S(1)}, u32[]{:S(2)}, u32[]{:S(2)}) collective-permute-start(f32[4,128,128]{2,1,0:T(8,128)S(1)} %get-tuple-element.63), channel_id=1, source_target_pairs={{0,128},{4,132},{8,136},{12,140},{16,144},{20,148},{24,152},{28,15... | collective-permute-start | bytes 786440 | tf_op jit(solution)/shard_map/ppermute | solution.py:32
  32.5 1.2 collective-permute-start.12
  33.7 4.8 %collective-permute-done.3 = f32[4,128,128]{2,1,0:T(8,128)S(1)} collective-permute-done((f32[4,128,128]{2,1,0:T(8,128)S(1)}, f32[4,128,128]{2,1,0:T(8,128)S(1)}, u32[]{:S(2)}, u32[]{:S(2)}) %collective-permute-start.3) | collective-permute-done | bytes 262176 | tf_op jit(solution)/shard_map/ppermute | solution.py:32
  39.0 1.3 collective-permute-start.8
  40.3 1.5 collective-permute-start.6
  43.3 2.1 collective-permute-start.13
  47.0 11.9 %panel.1 = (bf16[4,4,4,512,128]{4,3,2,1,0:T(8,128)(2,1)S(1)}, bf16[4,4,4,512,128]{4,3,2,1,0:T(8,128)(2,1)S(1)}) custom-call(s32[3]{0:T(128)S(1)} %pad_add_fusion.at_ref, s32[64]{0:T(128)S(1)} %bitcast.102, s32[128]{0:T(128)S(1)} %reshape.22.block_ref, f32[4,4,4,2,128,128]{5,4,3,2,1,0:T(8,128)} %bitcast.103), custom_call_target="tpu_custom_call" | custom-call | flops 100000000 | bytes 25000000 | tf_op jit(solution)/shard_map/panel/pallas_call | solution.py:67
  59.0 3.3 %copy-done = bf16[4,4,4,512,128]{4,3,2,1,0:T(8,128)(2,1)} copy-done((bf16[4,4,4,512,128]{4,3,2,1,0:T(8,128)(2,1)}, bf16[4,4,4,512,128]{4,3,2,1,0:T(8,128)(2,1)S(1)}, u32[]{:S(2)}) %copy-start) | copy-done | bytes 8388632
  62.3 3.3 %copy-done.1 = bf16[4,4,4,512,128]{4,3,2,1,0:T(8,128)(2,1)} copy-done((bf16[4,4,4,512,128]{4,3,2,1,0:T(8,128)(2,1)}, bf16[4,4,4,512,128]{4,3,2,1,0:T(8,128)(2,1)S(1)}, u32[]{:S(2)}) %copy-start.1) | copy-done | bytes 8388632
  65.6 2.2 collective-permute-start.9
  69.0 1.4 collective-permute-start.7
  72.8 2.7 %collective-permute-start.14 = (f32[2,4,128,128]{3,2,1,0:T(8,128)S(1)}, f32[2,4,128,128]{3,2,1,0:T(8,128)S(1)}, u32[]{:S(2)}, u32[]{:S(2)}) collective-permute-start(f32[2,4,128,128]{3,2,1,0:T(8,128)S(1)} %slice.136), channel_id=1, source_target_pairs={{0,12},{4,0},{8,4},{12,8},{16,28},{20,16},{24,20},{28,24},{32,44},... | collective-permute-start | bytes 1572872 | tf_op jit(solution)/shard_map/ppermute | solution.py:32
  75.6 6.0 %forward.3 = (f32[512,128]{1,0:T(8,128)S(1)}, f32[512,128]{1,0:T(8,128)S(1)}) custom-call(bf16[4,4,4,512,128]{4,3,2,1,0:T(8,128)(2,1)} %copy-done, bf16[4,4,4,512,128]{4,3,2,1,0:T(8,128)(2,1)} %copy-done, bf16[4,4,4,512,128]{4,3,2,1,0:T(8,128)(2,1)} %copy-done.1, bf16[4,4,4,512,128]{4,3,2,1,0:T(8,128)(2,1)} %copy-done.1, ...), custom_call_target="tpu_custom_call" | custom-call | flops 2147483648 | bytes 10400000 | tf_op jit(solution)/shard_map/forward/pallas_call | solution.py:125
  81.6 9.0 %forward.4 = (f32[512,128]{1,0:T(8,128)S(1)}, f32[512,128]{1,0:T(8,128)S(1)}) custom-call(bf16[4,4,4,512,128]{4,3,2,1,0:T(8,128)(2,1)} %copy-done, bf16[4,4,4,512,128]{4,3,2,1,0:T(8,128)(2,1)} %copy-done, bf16[4,4,4,512,128]{4,3,2,1,0:T(8,128)(2,1)} %copy-done, bf16[4,4,4,512,128]{4,3,2,1,0:T(8,128)(2,1)} %copy-done, bf16[4,4,4,512,128]{4,3,2,1,0:T(8,128)(2,1)} %copy-done.1, ...), custom_call_target="tpu_custom_call" | custom-call | flops 4294967296 | bytes 20800000 | tf_op jit(solution)/shard_map/forward/pallas_call | solution.py:125
  90.7 5.9 %forward.5 = (f32[512,128]{1,0:T(8,128)S(1)}, f32[512,128]{1,0:T(8,128)S(1)}) custom-call(bf16[4,4,4,512,128]{4,3,2,1,0:T(8,128)(2,1)} %copy-done, bf16[4,4,4,512,128]{4,3,2,1,0:T(8,128)(2,1)} %copy-done, bf16[4,4,4,512,128]{4,3,2,1,0:T(8,128)(2,1)} %copy-done, bf16[4,4,4,512,128]{4,3,2,1,0:T(8,128)(2,1)} %copy-done, bf16[4,4,4,512,128]{4,3,2,1,0:T(8,128)(2,1)} %copy-done.1, ...), custom_call_target="tpu_custom_call" | custom-call | flops 2147483648 | bytes 10400000 | tf_op jit(solution)/shard_map/forward/pallas_call | solution.py:125
  96.7 3.2 %collective-permute-start.17 = (f32[2,128,256]{2,1,0:T(8,128)S(1)}, f32[2,128,256]{2,1,0:T(8,128)S(1)}, u32[]{:S(2)}, u32[]{:S(2)}) collective-permute-start(f32[2,128,256]{2,1,0:T(8,128)S(1)} %dynamic-slice_bitcast_fusion), channel_id=1, source_target_pairs={{0,1},{1,0},{2,3},{3,2},{4,5},{5,4},{6,7},{7,6},{8,9},{9,8},{10,11... | collective-permute-start | bytes 786440 | tf_op jit(solution)/shard_map/ppermute | solution.py:36
  99.8 1.2 collective-permute-done.17
  101.2 4.7 %collective-permute-done.18.other_ref = f32[128,256]{1,0:T(8,128)S(1)} collective-permute-done((f32[128,256]{1,0:T(8,128)S(1)}, f32[128,256]{1,0:T(8,128)S(1)}, u32[]{:S(2)}, u32[]{:S(2)}) %collective-permute-start.18) | collective-permute-done | bytes 131104 | tf_op jit(solution)/shard_map/ppermute | solution.py:36
  107.0 1.3 collective-permute-start.19
  108.2 7.3 %all-gather = f32[1024,128]{1,0:T(8,128)S(1)} all-gather(f32[256,128]{1,0:T(8,128)S(1)} %get-tuple-element.36), channel_id=2, replica_groups=mesh['rows'=64,'rep'=4] {'rep'}, dimensions={0}, use_global_device_ids=true | all-gather | bytes 655360 | tf_op jit(solution)/shard_map/all_gather | solution.py:298
  115.7 8.7 %backward.3 = (f32[4,4,128,128]{3,2,1,0:T(8,128)S(1)}, f32[4,4,128,128]{3,2,1,0:T(8,128)S(1)}, f32[4,4,128,128]{3,2,1,0:T(8,128)S(1)}, f32[4,4,128,128]{3,2,1,0:T(8,128)S(1)}) custom-call(f32[4,256,128]{2,1,0:T(8,128)S(1)} %bitcast.98, bf16[4,4,4,512,128]{4,3,2,1,0:T(8,128)(2,1)} %copy-done, bf16[4,4,4,512,128]{4,3,2,1,0:T(8,128)(2,1)} %copy-done, ...), custom_call_target="tpu_custom_call" | custom-call | flops 4294967296 | bytes 20800000 | tf_op jit(solution)/shard_map/backward/pallas_call | solution.py:185
  125.4 3.4 %collective-permute-start.23 = (f32[64,256]{1,0:T(8,128)S(1)}, f32[64,256]{1,0:T(8,128)S(1)}, u32[]{:S(2)}, u32[]{:S(2)}) collective-permute-start(f32[64,256]{1,0:T(8,128)S(1)} %bitcast_add_fusion.2), channel_id=1, source_target_pairs={{0,48},{4,52},{8,56},{12,60},{16,0},{20,4},{24,8},{28,12},{32,16},... | collective-permute-start | bytes 196616 | tf_op jit(solution)/shard_map/ppermute | solution.py:32
  128.8 3.1 %collective-permute-start.21 = (f32[64,256]{1,0:T(8,128)S(1)}, f32[64,256]{1,0:T(8,128)S(1)}, u32[]{:S(2)}, u32[]{:S(2)}) collective-permute-start(f32[64,256]{1,0:T(8,128)S(1)} %bitcast_add_fusion.2), channel_id=1, source_target_pairs={{0,32},{4,36},{8,40},{12,44},{16,48},{20,52},{24,56},{28,60},{32,0... | collective-permute-start | bytes 196616 | tf_op jit(solution)/shard_map/ppermute | solution.py:32
  132.0 2.8 %collective-permute-done.22 = f32[64,256]{1,0:T(8,128)S(1)} collective-permute-done((f32[64,256]{1,0:T(8,128)S(1)}, f32[64,256]{1,0:T(8,128)S(1)}, u32[]{:S(2)}, u32[]{:S(2)}) %collective-permute-start.22) | collective-permute-done | bytes 65568 | tf_op jit(solution)/shard_map/ppermute | solution.py:32
  134.7 1.8 collective-permute-done.21
  136.6 10.6 %collective-permute-start.30 = (f32[4,4,128,128]{3,2,1,0:T(8,128)S(1)}, f32[4,4,128,128]{3,2,1,0:T(8,128)S(1)}, u32[]{:S(2)}, u32[]{:S(2)}) collective-permute-start(f32[4,4,128,128]{3,2,1,0:T(8,128)S(1)} %get-tuple-element.38), channel_id=1, source_target_pairs={{0,192},{4,196},{8,200},{12,204},{16,208},{20,212},{24,216},{28,22... | collective-permute-start | bytes 3145736 | tf_op jit(solution)/shard_map/ppermute | solution.py:32
  148.4 2.7 %collective-permute-start.24 = (f32[64,256]{1,0:T(8,128)S(1)}, f32[64,256]{1,0:T(8,128)S(1)}, u32[]{:S(2)}, u32[]{:S(2)}) collective-permute-start(f32[64,256]{1,0:T(8,128)S(1)} %add_add_fusion.2), channel_id=1, source_target_pairs={{0,8},{4,12},{8,0},{12,4},{16,24},{20,28},{24,16},{28,20},{32,40},... | collective-permute-start | bytes 196616 | tf_op jit(solution)/shard_map/ppermute | solution.py:32
  151.1 9.1 %backward.2 = (f32[2,4,128,128]{3,2,1,0:T(8,128)S(1)}, f32[2,4,128,128]{3,2,1,0:T(8,128)S(1)}, f32[2,4,128,128]{3,2,1,0:T(8,128)S(1)}, f32[2,4,128,128]{3,2,1,0:...) custom-call(f32[4,256,128]{2,1,0:T(8,128)S(1)} %bitcast.99, ...), custom_call_target="tpu_custom_call" | custom-call | flops 4294967296 | bytes 20800000 | tf_op jit(solution)/shard_map/backward/pallas_call | solution.py:185
  160.1 12.3 %collective-permute-done.25 = f32[64,256]{1,0:T(8,128)S(1)} collective-permute-done((f32[64,256]{1,0:T(8,128)S(1)}, f32[64,256]{1,0:T(8,128)S(1)}, u32[]{:S(2)}, u32[]{:S(2)}) %collective-permute-start.25) | collective-permute-done | bytes 65568 | tf_op jit(solution)/shard_map/ppermute | solution.py:32
  174.6 1.3 collective-permute-done.29
  177.3 1.4 collective-permute-done.27
  178.9 9.3 %collective-permute-done.32 = f32[2,4,128,128]{3,2,1,0:T(8,128)S(1)} collective-permute-done((f32[2,4,128,128]{3,2,1,0:T(8,128)S(1)}, f32[2,4,128,128]{3,2,1,0:T(8,128)S(1)}, u32[]{:S(2)}, u32[]{:S(2)}) %collective-permute-start.32) | collective-permute-done | bytes 524320 | tf_op jit(solution)/shard_map/ppermute | solution.py:32
  188.7 7.0 %collective-permute-done.37 = f32[4,4,128,128]{3,2,1,0:T(8,128)S(1)} collective-permute-done((f32[4,4,128,128]{3,2,1,0:T(8,128)S(1)}, f32[4,4,128,128]{3,2,1,0:T(8,128)S(1)}, u32[]{:S(2)}, u32[]{:S(2)}) %collective-permute-start.37) | collective-permute-done | bytes 1048608 | tf_op jit(solution)/shard_map/ppermute | solution.py:32
  195.9 1.6 collective-permute-start.41
  197.7 1.9 collective-permute-start.35
  199.6 1.7 collective-permute-start.36
  201.3 6.5 %collective-permute-done.41 = f32[2,4,128,128]{3,2,1,0:T(8,128)S(1)} collective-permute-done((f32[2,4,128,128]{3,2,1,0:T(8,128)S(1)}, f32[2,4,128,128]{3,2,1,0:T(8,128)S(1)}, u32[]{:S(2)}, u32[]{:S(2)}) %collective-permute-start.41) | collective-permute-done | bytes 524320 | tf_op jit(solution)/shard_map/ppermute | solution.py:32
  207.9 1.3 collective-permute-start.42
  210.3 18.1 %all_gather.9 = f32[256,256]{1,0:T(8,128)S(1)} all-gather(f32[64,256]{1,0:T(8,128)S(1)} %add_add_fusion), channel_id=1, replica_groups=mesh['rows'=64,'rep'=4] {'rep'}, dimensions={0}, use_global_device_ids=true | all-gather | bytes 327680 | tf_op jit(solution)/shard_map/all_gather | solution.py:305
  228.6 5.5 %collective-permute-start.44 = (f32[2,128,128]{2,1,0:T(8,128)S(1)}, f32[2,128,128]{2,1,0:T(8,128)S(1)}, u32[]{:S(2)}, u32[]{:S(2)}) collective-permute-start(f32[2,128,128]{2,1,0:T(8,128)S(1)} %get-tuple-element.53), channel_id=1, source_target_pairs={{0,16},{4,20},{8,24},{12,28},{16,32},{20,36},{24,40},{28,44},{32,4... | collective-permute-start | bytes 393224 | tf_op jit(solution)/shard_map/ppermute | solution.py:32
  234.1 3.4 %collective-permute-start.45 = (f32[2,128,128]{2,1,0:T(8,128)S(1)}, f32[2,128,128]{2,1,0:T(8,128)S(1)}, u32[]{:S(2)}, u32[]{:S(2)}) collective-permute-start(f32[2,128,128]{2,1,0:T(8,128)S(1)} %get-tuple-element.55), channel_id=1, source_target_pairs={{0,32},{4,36},{8,40},{12,44},{16,48},{20,52},{24,56},{28,60},{32,0... | collective-permute-start | bytes 393224 | tf_op jit(solution)/shard_map/ppermute | solution.py:32
  238.7 10.1 %collective-permute-done.46 = f32[2,128,128]{2,1,0:T(8,128)S(1)} collective-permute-done((f32[2,128,128]{2,1,0:T(8,128)S(1)}, f32[2,128,128]{2,1,0:T(8,128)S(1)}, u32[]{:S(2)}, u32[]{:S(2)}) %collective-permute-start.46) | collective-permute-done | bytes 131104 | tf_op jit(solution)/shard_map/ppermute | solution.py:32
  (109 shorter events, 22.9 us)
Async XLA Ops:
  1.5 11.4 %collective-permute-start.2 = (f32[2,128,128]{2,1,0:T(8,128)S(1)}, f32[2,128,128]{2,1,0:T(8,128)S(1)}, u32[]{:S(2)}, u32[]{:S(2)}) collective-permute-start(f32[2,128,128]{2,1,0:T(8,128)S(1)} %pad_maximum_fusion.6), channel_id=1, source_target_pairs={{0,16},{4,20},{8,24},{12,28},{16,32},{20,36},{24,40},{28,44},{32,4... | collective-permute-start | bytes 393224 | tf_op jit(solution)/shard_map/ppermute | solution.py:32
  5.4 13.7 %collective-permute-start.1 = (f32[2,128,128]{2,1,0:T(8,128)S(1)}, f32[2,128,128]{2,1,0:T(8,128)S(1)}, u32[]{:S(2)}, u32[]{:S(2)}) collective-permute-start(f32[2,128,128]{2,1,0:T(8,128)S(1)} %pad_maximum_fusion.6), channel_id=1, source_target_pairs={{0,32},{4,36},{8,40},{12,44},{16,48},{20,52},{24,56},{28,60},{32,0... | collective-permute-start | bytes 393224 | tf_op jit(solution)/shard_map/ppermute | solution.py:32
  10.5 12.9 %collective-permute-start = (f32[2,128,128]{2,1,0:T(8,128)S(1)}, f32[2,128,128]{2,1,0:T(8,128)S(1)}, u32[]{:S(2)}, u32[]{:S(2)}) collective-permute-start(f32[2,128,128]{2,1,0:T(8,128)S(1)} %pad_maximum_fusion.6), channel_id=1, source_target_pairs={{0,48},{4,52},{8,56},{12,60},{16,0},{20,4},{24,8},{28,12},{32,16},... | collective-permute-start | bytes 393224 | tf_op jit(solution)/shard_map/ppermute | solution.py:32
  23.5 9.0 %collective-permute-start.4 = (f32[4,128,128]{2,1,0:T(8,128)S(1)}, f32[4,128,128]{2,1,0:T(8,128)S(1)}, u32[]{:S(2)}, u32[]{:S(2)}) collective-permute-start(f32[4,128,128]{2,1,0:T(8,128)S(1)} %get-tuple-element.65), channel_id=1, source_target_pairs={{0,8},{4,12},{8,0},{12,4},{16,24},{20,28},{24,16},{28,20},{32,40},... | collective-permute-start | bytes 786440 | tf_op jit(solution)/shard_map/ppermute | solution.py:32
  26.5 12.0 %collective-permute-start.3 = (f32[4,128,128]{2,1,0:T(8,128)S(1)}, f32[4,128,128]{2,1,0:T(8,128)S(1)}, u32[]{:S(2)}, u32[]{:S(2)}) collective-permute-start(f32[4,128,128]{2,1,0:T(8,128)S(1)} %get-tuple-element.65), channel_id=1, source_target_pairs={{0,12},{4,0},{8,4},{12,8},{16,28},{20,16},{24,20},{28,24},{32,44},... | collective-permute-start | bytes 786440 | tf_op jit(solution)/shard_map/ppermute | solution.py:32
  27.3 11.6 %collective-permute-start.5 = (f32[4,128,128]{2,1,0:T(8,128)S(1)}, f32[4,128,128]{2,1,0:T(8,128)S(1)}, u32[]{:S(2)}, u32[]{:S(2)}) collective-permute-start(f32[4,128,128]{2,1,0:T(8,128)S(1)} %get-tuple-element.65), channel_id=1, source_target_pairs={{0,4},{4,8},{8,12},{12,0},{16,20},{20,24},{24,28},{28,16},{32,36},... | collective-permute-start | bytes 786440 | tf_op jit(solution)/shard_map/ppermute | solution.py:32
  28.0 13.7 %collective-permute-start.11 = (f32[4,128,128]{2,1,0:T(8,128)S(1)}, f32[4,128,128]{2,1,0:T(8,128)S(1)}, u32[]{:S(2)}, u32[]{:S(2)}) collective-permute-start(f32[4,128,128]{2,1,0:T(8,128)S(1)} %get-tuple-element.63), channel_id=1, source_target_pairs={{0,128},{4,132},{8,136},{12,140},{16,144},{20,148},{24,152},{28,15... | collective-permute-start | bytes 786440 | tf_op jit(solution)/shard_map/ppermute | solution.py:32
  30.9 11.7 %collective-permute-start.10 = (f32[4,128,128]{2,1,0:T(8,128)S(1)}, f32[4,128,128]{2,1,0:T(8,128)S(1)}, u32[]{:S(2)}, u32[]{:S(2)}) collective-permute-start(f32[4,128,128]{2,1,0:T(8,128)S(1)} %get-tuple-element.63), channel_id=1, source_target_pairs={{0,192},{4,196},{8,200},{12,204},{16,208},{20,212},{24,216},{28,22... | collective-permute-start | bytes 786440 | tf_op jit(solution)/shard_map/ppermute | solution.py:32
  32.5 10.0 %collective-permute-start.12 = (f32[4,128,128]{2,1,0:T(8,128)S(1)}, f32[4,128,128]{2,1,0:T(8,128)S(1)}, u32[]{:S(2)}, u32[]{:S(2)}) collective-permute-start(f32[4,128,128]{2,1,0:T(8,128)S(1)} %get-tuple-element.63), channel_id=1, source_target_pairs={{0,64},{4,68},{8,72},{12,76},{16,80},{20,84},{24,88},{28,92},{32,9... | collective-permute-start | bytes 786440 | tf_op jit(solution)/shard_map/ppermute | solution.py:32
  39.0 26.6 %collective-permute-start.8 = (f32[4,4,128,128]{3,2,1,0:T(8,128)S(1)}, f32[4,4,128,128]{3,2,1,0:T(8,128)S(1)}, u32[]{:S(2)}, u32[]{:S(2)}) collective-permute-start(f32[4,4,128,128]{3,2,1,0:T(8,128)S(1)} %pad_maximum_fusion.refs_4_), channel_id=1, source_target_pairs={{0,64},{4,68},{8,72},{12,76},{16,80},{20,84},{24,88},{28,92},{32,9... | collective-permute-start | bytes 3145736 | tf_op jit(solution)/shard_map/ppermute | solution.py:32
  40.3 27.6 %collective-permute-start.6 = (f32[4,4,128,128]{3,2,1,0:T(8,128)S(1)}, f32[4,4,128,128]{3,2,1,0:T(8,128)}, u32[]{:S(2)}, u32[]{:S(2)}) collective-permute-start(f32[4,4,128,128]{3,2,1,0:T(8,128)S(1)} %pad_maximum_fusion.refs_4_), channel_id=1, source_target_pairs={{0,192},{4,196},{8,200},{12,204},{16,208},{20,212},{24,216},{28,22... | collective-permute-start | bytes 3145736 | tf_op jit(solution)/shard_map/ppermute | solution.py:32
  42.6 27.7 %collective-permute-start.15 = (f32[4,4,128,128]{3,2,1,0:T(8,128)S(1)}, f32[4,4,128,128]{3,2,1,0:T(8,128)}, u32[]{:S(2)}, u32[]{:S(2)}) collective-permute-start(f32[4,4,128,128]{3,2,1,0:T(8,128)S(1)} %pad_maximum_fusion.1.refs_5_), channel_id=1, source_target_pairs={{0,4},{4,8},{8,12},{12,0},{16,20},{20,24},{24,28},{28,16},{32,36},... | collective-permute-start | bytes 3145736 | tf_op jit(solution)/shard_map/ppermute | solution.py:32
  43.3 28.5 %collective-permute-start.13 = (f32[4,4,128,128]{3,2,1,0:T(8,128)S(1)}, f32[4,4,128,128]{3,2,1,0:T(8,128)}, u32[]{:S(2)}, u32[]{:S(2)}) collective-permute-start(f32[4,4,128,128]{3,2,1,0:T(8,128)S(1)} %pad_maximum_fusion.1.refs_5_), channel_id=1, source_target_pairs={{0,12},{4,0},{8,4},{12,8},{16,28},{20,16},{24,20},{28,24},{32,44},... | collective-permute-start | bytes 3145736 | tf_op jit(solution)/shard_map/ppermute | solution.py:32
  65.6 25.0 %collective-permute-start.9 = (f32[2,4,128,128]{3,2,1,0:T(8,128)S(1)}, f32[2,4,128,128]{3,2,1,0:T(8,128)S(1)}, u32[]{:S(2)}, u32[]{:S(2)}) collective-permute-start(f32[2,4,128,128]{3,2,1,0:T(8,128)S(1)} %slice.132), channel_id=1, source_target_pairs={{0,64},{4,68},{8,72},{12,76},{16,80},{20,84},{24,88},{28,92},{32,9... | collective-permute-start | bytes 1572872 | tf_op jit(solution)/shard_map/ppermute | solution.py:32
  69.0 21.7 %collective-permute-start.7 = (f32[2,4,128,128]{3,2,1,0:T(8,128)S(1)}, f32[2,4,128,128]{3,2,1,0:T(8,128)S(1)}, u32[]{:S(2)}, u32[]{:S(2)}) collective-permute-start(f32[2,4,128,128]{3,2,1,0:T(8,128)S(1)} %slice.131), channel_id=1, source_target_pairs={{0,192},{4,196},{8,200},{12,204},{16,208},{20,212},{24,216},{28,22... | collective-permute-start | bytes 1572872 | tf_op jit(solution)/shard_map/ppermute | solution.py:32
  71.4 19.3 %collective-permute-start.16 = (f32[2,4,128,128]{3,2,1,0:T(8,128)S(1)}, f32[2,4,128,128]{3,2,1,0:T(8,128)S(1)}, u32[]{:S(2)}, u32[]{:S(2)}) collective-permute-start(f32[2,4,128,128]{3,2,1,0:T(8,128)S(1)} %slice.137), channel_id=1, source_target_pairs={{0,4},{4,8},{8,12},{12,0},{16,20},{20,24},{24,28},{28,16},{32,36},... | collective-permute-start | bytes 1572872 | tf_op jit(solution)/shard_map/ppermute | solution.py:32
  72.8 17.8 %collective-permute-start.14 = (f32[2,4,128,128]{3,2,1,0:T(8,128)S(1)}, f32[2,4,128,128]{3,2,1,0:T(8,128)S(1)}, u32[]{:S(2)}, u32[]{:S(2)}) collective-permute-start(f32[2,4,128,128]{3,2,1,0:T(8,128)S(1)} %slice.136), channel_id=1, source_target_pairs={{0,12},{4,0},{8,4},{12,8},{16,28},{20,16},{24,20},{28,24},{32,44},... | collective-permute-start | bytes 1572872 | tf_op jit(solution)/shard_map/ppermute | solution.py:32
  90.7 15.2 %copy-start.2 = (f32[256,256]{1,0:T(8,128)S(1)}, f32[256,256]{1,0:T(8,128)}, u32[]{:S(2)}) copy-start(f32[256,256]{1,0:T(8,128)} %weight_ref.1) | copy-start | bytes 786436
  96.7 4.4 %collective-permute-start.17 = (f32[2,128,256]{2,1,0:T(8,128)S(1)}, f32[2,128,256]{2,1,0:T(8,128)S(1)}, u32[]{:S(2)}, u32[]{:S(2)}) collective-permute-start(f32[2,128,256]{2,1,0:T(8,128)S(1)} %dynamic-slice_bitcast_fusion), channel_id=1, source_target_pairs={{0,1},{1,0},{2,3},{3,2},{4,5},{5,4},{6,7},{7,6},{8,9},{9,8},{10,11... | collective-permute-start | bytes 786440 | tf_op jit(solution)/shard_map/ppermute | solution.py:36
  101.1 4.8 %collective-permute-start.18 = (f32[128,256]{1,0:T(8,128)S(1)}, f32[128,256]{1,0:T(8,128)S(1)}, u32[]{:S(2)}, u32[]{:S(2)}) collective-permute-start(f32[128,256]{1,0:T(8,128)S(1)} %get-tuple-element.60), channel_id=1, source_target_pairs={{0,2},{1,3},{2,0},{3,1},{4,6},{5,7},{6,4},{7,5},{8,10},{9,11},{10,... | collective-permute-start | bytes 393224 | tf_op jit(solution)/shard_map/ppermute | solution.py:36
  107.0 8.6 %collective-permute-start.19 = (f32[2,64,256]{2,1,0:T(8,128)S(1)}, f32[2,64,256]{2,1,0:T(8,128)S(1)}, u32[]{:S(2)}, u32[]{:S(2)}) collective-permute-start(f32[2,64,256]{2,1,0:T(8,128)S(1)} %dynamic-slice_bitcast_fusion.1), channel_id=1, source_target_pairs={{0,1},{1,0},{2,3},{3,2},{4,5},{5,4},{6,7},{7,6},{8,9},{9,8},{10,11... | collective-permute-start | bytes 393224 | tf_op jit(solution)/shard_map/ppermute | solution.py:36
  115.6 9.8 %collective-permute-start.20 = (f32[64,256]{1,0:T(8,128)S(1)}, f32[64,256]{1,0:T(8,128)S(1)}, u32[]{:S(2)}, u32[]{:S(2)}) collective-permute-start(f32[64,256]{1,0:T(8,128)S(1)} %dynamic-slice_bitcast_fusion.4), channel_id=1, source_target_pairs={{0,2},{1,3},{2,0},{3,1},{4,6},{5,7},{6,4},{7,5},{8,10},{9,11},{10,... | collective-permute-start | bytes 196616 | tf_op jit(solution)/shard_map/ppermute | solution.py:36
  124.3 49.7 %collective-permute-start.31 = (f32[4,4,128,128]{3,2,1,0:T(8,128)S(1)}, f32[4,4,128,128]{3,2,1,0:T(8,128)S(1)}, u32[]{:S(2)}, u32[]{:S(2)}) collective-permute-start(f32[4,4,128,128]{3,2,1,0:T(8,128)S(1)} %get-tuple-element.40), channel_id=1, source_target_pairs={{0,64},{4,68},{8,72},{12,76},{16,80},{20,84},{24,88},{28,92},{32,9... | collective-permute-start | bytes 3145736 | tf_op jit(solution)/shard_map/ppermute | solution.py:32
  125.4 6.5 %collective-permute-start.23 = (f32[64,256]{1,0:T(8,128)S(1)}, f32[64,256]{1,0:T(8,128)S(1)}, u32[]{:S(2)}, u32[]{:S(2)}) collective-permute-start(f32[64,256]{1,0:T(8,128)S(1)} %bitcast_add_fusion.2), channel_id=1, source_target_pairs={{0,48},{4,52},{8,56},{12,60},{16,0},{20,4},{24,8},{28,12},{32,16},... | collective-permute-start | bytes 196616 | tf_op jit(solution)/shard_map/ppermute | solution.py:32
  128.8 5.9 %collective-permute-start.22 = (f32[64,256]{1,0:T(8,128)S(1)}, f32[64,256]{1,0:T(8,128)S(1)}, u32[]{:S(2)}, u32[]{:S(2)}) collective-permute-start(f32[64,256]{1,0:T(8,128)S(1)} %bitcast_add_fusion.2), channel_id=1, source_target_pairs={{0,16},{4,20},{8,24},{12,28},{16,32},{20,36},{24,40},{28,44},{32,4... | collective-permute-start | bytes 196616 | tf_op jit(solution)/shard_map/ppermute | solution.py:32
  128.8 7.7 %collective-permute-start.21 = (f32[64,256]{1,0:T(8,128)S(1)}, f32[64,256]{1,0:T(8,128)S(1)}, u32[]{:S(2)}, u32[]{:S(2)}) collective-permute-start(f32[64,256]{1,0:T(8,128)S(1)} %bitcast_add_fusion.2), channel_id=1, source_target_pairs={{0,32},{4,36},{8,40},{12,44},{16,48},{20,52},{24,56},{28,60},{32,0... | collective-permute-start | bytes 196616 | tf_op jit(solution)/shard_map/ppermute | solution.py:32
  136.5 11.8 %collective-permute-start.26 = (f32[64,256]{1,0:T(8,128)S(1)}, f32[64,256]{1,0:T(8,128)S(1)}, u32[]{:S(2)}, u32[]{:S(2)}) collective-permute-start(f32[64,256]{1,0:T(8,128)S(1)} %add_add_fusion.2), channel_id=1, source_target_pairs={{0,12},{4,0},{8,4},{12,8},{16,28},{20,16},{24,20},{28,24},{32,44},... | collective-permute-start | bytes 196616 | tf_op jit(solution)/shard_map/ppermute | solution.py:32
  136.6 42.3 %collective-permute-start.30 = (f32[4,4,128,128]{3,2,1,0:T(8,128)S(1)}, f32[4,4,128,128]{3,2,1,0:T(8,128)S(1)}, u32[]{:S(2)}, u32[]{:S(2)}) collective-permute-start(f32[4,4,128,128]{3,2,1,0:T(8,128)S(1)} %get-tuple-element.38), channel_id=1, source_target_pairs={{0,192},{4,196},{8,200},{12,204},{16,208},{20,212},{24,216},{28,22... | collective-permute-start | bytes 3145736 | tf_op jit(solution)/shard_map/ppermute | solution.py:32
  147.2 31.5 %collective-permute-start.38 = (f32[4,4,128,128]{3,2,1,0:T(8,128)S(1)}, f32[4,4,128,128]{3,2,1,0:T(8,128)S(1)}, u32[]{:S(2)}, u32[]{:S(2)}) collective-permute-start(f32[4,4,128,128]{3,2,1,0:T(8,128)S(1)} %get-tuple-element.46), channel_id=1, source_target_pairs={{0,4},{4,8},{8,12},{12,0},{16,20},{20,24},{24,28},{28,16},{32,36},... | collective-permute-start | bytes 3145736 | tf_op jit(solution)/shard_map/ppermute | solution.py:32
  148.3 24.2 %collective-permute-start.25 = (f32[64,256]{1,0:T(8,128)S(1)}, f32[64,256]{1,0:T(8,128)S(1)}, u32[]{:S(2)}, u32[]{:S(2)}) collective-permute-start(f32[64,256]{1,0:T(8,128)S(1)} %add_add_fusion.2), channel_id=1, source_target_pairs={{0,4},{4,8},{8,12},{12,0},{16,20},{20,24},{24,28},{28,16},{32,36},... | collective-permute-start | bytes 196616 | tf_op jit(solution)/shard_map/ppermute | solution.py:32
  148.4 24.1 %collective-permute-start.24 = (f32[64,256]{1,0:T(8,128)S(1)}, f32[64,256]{1,0:T(8,128)S(1)}, u32[]{:S(2)}, u32[]{:S(2)}) collective-permute-start(f32[64,256]{1,0:T(8,128)S(1)} %add_add_fusion.2), channel_id=1, source_target_pairs={{0,8},{4,12},{8,0},{12,4},{16,24},{20,28},{24,16},{28,20},{32,40},... | collective-permute-start | bytes 196616 | tf_op jit(solution)/shard_map/ppermute | solution.py:32
  172.5 3.5 %collective-permute-start.29 = (f32[64,256]{1,0:T(8,128)S(1)}, f32[64,256]{1,0:T(8,128)S(1)}, u32[]{:S(2)}, u32[]{:S(2)}) collective-permute-start(f32[64,256]{1,0:T(8,128)S(1)} %add_add_fusion.1), channel_id=1, source_target_pairs={{0,192},{4,196},{8,200},{12,204},{16,208},{20,212},{24,216},{28,22... | collective-permute-start | bytes 196616 | tf_op jit(solution)/shard_map/ppermute | solution.py:32
  172.9 4.3 %collective-permute-start.28 = (f32[64,256]{1,0:T(8,128)S(1)}, f32[64,256]{1,0:T(8,128)S(1)}, u32[]{:S(2)}, u32[]{:S(2)}) collective-permute-start(f32[64,256]{1,0:T(8,128)S(1)} %add_add_fusion.1), channel_id=1, source_target_pairs={{0,64},{4,68},{8,72},{12,76},{16,80},{20,84},{24,88},{28,92},{32,9... | collective-permute-start | bytes 196616 | tf_op jit(solution)/shard_map/ppermute | solution.py:32
  174.0 4.6 %collective-permute-start.27 = (f32[64,256]{1,0:T(8,128)S(1)}, f32[64,256]{1,0:T(8,128)S(1)}, u32[]{:S(2)}, u32[]{:S(2)}) collective-permute-start(f32[64,256]{1,0:T(8,128)S(1)} %add_add_fusion.1), channel_id=1, source_target_pairs={{0,128},{4,132},{8,136},{12,140},{16,144},{20,148},{24,152},{28,15... | collective-permute-start | bytes 196616 | tf_op jit(solution)/shard_map/ppermute | solution.py:32
  176.0 12.3 %collective-permute-start.32 = (f32[2,4,128,128]{3,2,1,0:T(8,128)S(1)}, f32[2,4,128,128]{3,2,1,0:T(8,128)S(1)}, u32[]{:S(2)}, u32[]{:S(2)}) collective-permute-start(f32[2,4,128,128]{3,2,1,0:T(8,128)S(1)} %slice_add_fusion.6), channel_id=1, source_target_pairs={{0,64},{4,68},{8,72},{12,76},{16,80},{20,84},{24,88},{28,92},{32,9... | collective-permute-start | bytes 1572872 | tf_op jit(solution)/shard_map/ppermute | solution.py:32
  177.3 18.4 %collective-permute-start.37 = (f32[4,4,128,128]{3,2,1,0:T(8,128)S(1)}, f32[4,4,128,128]{3,2,1,0:T(8,128)S(1)}, u32[]{:S(2)}, u32[]{:S(2)}) collective-permute-start(f32[4,4,128,128]{3,2,1,0:T(8,128)S(1)} %get-tuple-element.44), channel_id=1, source_target_pairs={{0,12},{4,0},{8,4},{12,8},{16,28},{20,16},{24,20},{28,24},{32,44},... | collective-permute-start | bytes 3145736 | tf_op jit(solution)/shard_map/ppermute | solution.py:32
  178.8 16.9 %collective-permute-start.39 = (f32[2,4,128,128]{3,2,1,0:T(8,128)S(1)}, f32[2,4,128,128]{3,2,1,0:T(8,128)S(1)}, u32[]{:S(2)}, u32[]{:S(2)}) collective-permute-start(f32[2,4,128,128]{3,2,1,0:T(8,128)S(1)} %slice_add_fusion.2), channel_id=1, source_target_pairs={{0,4},{4,8},{8,12},{12,0},{16,20},{20,24},{24,28},{28,16},{32,36},... | collective-permute-start | bytes 1572872 | tf_op jit(solution)/shard_map/ppermute | solution.py:32
  188.4 20.7 %collective-permute-start.33 = (f32[4,128,128]{2,1,0:T(8,128)S(1)}, f32[4,128,128]{2,1,0:T(8,128)S(1)}, u32[]{:S(2)}, u32[]{:S(2)}) collective-permute-start(f32[4,128,128]{2,1,0:T(8,128)S(1)} %slice_bitcast_fusion.6), channel_id=1, source_target_pairs={{0,4},{4,8},{8,12},{12,0},{16,20},{20,24},{24,28},{28,16},{32,36},... | collective-permute-start | bytes 786440 | tf_op jit(solution)/shard_map/ppermute | solution.py:32
  188.5 9.0 %collective-permute-start.34 = (f32[2,4,128,128]{3,2,1,0:T(8,128)S(1)}, f32[2,4,128,128]{3,2,1,0:T(8,128)S(1)}, u32[]{:S(2)}, u32[]{:S(2)}) collective-permute-start(f32[2,4,128,128]{3,2,1,0:T(8,128)S(1)} %get-tuple-element.50), channel_id=1, source_target_pairs={{0,192},{4,196},{8,200},{12,204},{16,208},{20,212},{24,216},{28,22... | collective-permute-start | bytes 1572872 | tf_op jit(solution)/shard_map/ppermute | solution.py:32
  195.9 11.9 %collective-permute-start.41 = (f32[2,4,128,128]{3,2,1,0:T(8,128)S(1)}, f32[2,4,128,128]{3,2,1,0:T(8,128)S(1)}, u32[]{:S(2)}, u32[]{:S(2)}) collective-permute-start(f32[2,4,128,128]{3,2,1,0:T(8,128)S(1)} %get-tuple-element.52), channel_id=1, source_target_pairs={{0,12},{4,0},{8,4},{12,8},{16,28},{20,16},{24,20},{28,24},{32,44},... | collective-permute-start | bytes 1572872 | tf_op jit(solution)/shard_map/ppermute | solution.py:32
  197.4 31.0 %collective-permute-start.40 = (f32[4,128,128]{2,1,0:T(8,128)S(1)}, f32[4,128,128]{2,1,0:T(8,128)S(1)}, u32[]{:S(2)}, u32[]{:S(2)}) collective-permute-start(f32[4,128,128]{2,1,0:T(8,128)S(1)} %slice_bitcast_fusion.2), channel_id=1, source_target_pairs={{0,64},{4,68},{8,72},{12,76},{16,80},{20,84},{24,88},{28,92},{32,9... | collective-permute-start | bytes 786440 | tf_op jit(solution)/shard_map/ppermute | solution.py:32
  197.7 30.7 %collective-permute-start.35 = (f32[4,128,128]{2,1,0:T(8,128)S(1)}, f32[4,128,128]{2,1,0:T(8,128)S(1)}, u32[]{:S(2)}, u32[]{:S(2)}) collective-permute-start(f32[4,128,128]{2,1,0:T(8,128)S(1)} %get-tuple-element.56), channel_id=1, source_target_pairs={{0,8},{4,12},{8,0},{12,4},{16,24},{20,28},{24,16},{28,20},{32,40},... | collective-permute-start | bytes 786440 | tf_op jit(solution)/shard_map/ppermute | solution.py:32
  199.6 28.8 %collective-permute-start.36 = (f32[4,128,128]{2,1,0:T(8,128)S(1)}, f32[4,128,128]{2,1,0:T(8,128)S(1)}, u32[]{:S(2)}, u32[]{:S(2)}) collective-permute-start(f32[4,128,128]{2,1,0:T(8,128)S(1)} %get-tuple-element.57), channel_id=1, source_target_pairs={{0,12},{4,0},{8,4},{12,8},{16,28},{20,16},{24,20},{28,24},{32,44},... | collective-permute-start | bytes 786440 | tf_op jit(solution)/shard_map/ppermute | solution.py:32
  207.9 20.6 %collective-permute-start.42 = (f32[4,128,128]{2,1,0:T(8,128)S(1)}, f32[4,128,128]{2,1,0:T(8,128)S(1)}, u32[]{:S(2)}, u32[]{:S(2)}) collective-permute-start(f32[4,128,128]{2,1,0:T(8,128)S(1)} %get-tuple-element.58), channel_id=1, source_target_pairs={{0,128},{4,132},{8,136},{12,140},{16,144},{20,148},{24,152},{28,15... | collective-permute-start | bytes 786440 | tf_op jit(solution)/shard_map/ppermute | solution.py:32
  209.2 19.3 %collective-permute-start.43 = (f32[4,128,128]{2,1,0:T(8,128)S(1)}, f32[4,128,128]{2,1,0:T(8,128)S(1)}, u32[]{:S(2)}, u32[]{:S(2)}) collective-permute-start(f32[4,128,128]{2,1,0:T(8,128)S(1)} %get-tuple-element.59), channel_id=1, source_target_pairs={{0,192},{4,196},{8,200},{12,204},{16,208},{20,212},{24,216},{28,22... | collective-permute-start | bytes 786440 | tf_op jit(solution)/shard_map/ppermute | solution.py:32
  228.6 10.1 %collective-permute-start.44 = (f32[2,128,128]{2,1,0:T(8,128)S(1)}, f32[2,128,128]{2,1,0:T(8,128)S(1)}, u32[]{:S(2)}, u32[]{:S(2)}) collective-permute-start(f32[2,128,128]{2,1,0:T(8,128)S(1)} %get-tuple-element.53), channel_id=1, source_target_pairs={{0,16},{4,20},{8,24},{12,28},{16,32},{20,36},{24,40},{28,44},{32,4... | collective-permute-start | bytes 393224 | tf_op jit(solution)/shard_map/ppermute | solution.py:32
  234.1 14.7 %collective-permute-start.46 = (f32[2,128,128]{2,1,0:T(8,128)S(1)}, f32[2,128,128]{2,1,0:T(8,128)S(1)}, u32[]{:S(2)}, u32[]{:S(2)}) collective-permute-start(f32[2,128,128]{2,1,0:T(8,128)S(1)} %get-tuple-element.54), channel_id=1, source_target_pairs={{0,48},{4,52},{8,56},{12,60},{16,0},{20,4},{24,8},{28,12},{32,16},... | collective-permute-start | bytes 393224 | tf_op jit(solution)/shard_map/ppermute | solution.py:32
  234.1 14.7 %collective-permute-start.45 = (f32[2,128,128]{2,1,0:T(8,128)S(1)}, f32[2,128,128]{2,1,0:T(8,128)S(1)}, u32[]{:S(2)}, u32[]{:S(2)}) collective-permute-start(f32[2,128,128]{2,1,0:T(8,128)S(1)} %get-tuple-element.55), channel_id=1, source_target_pairs={{0,32},{4,36},{8,40},{12,44},{16,48},{20,52},{24,56},{28,60},{32,0... | collective-permute-start | bytes 393224 | tf_op jit(solution)/shard_map/ppermute | solution.py:32
  (4 other events, 22.5 us)
